TPU v7x, 512 devices: a whole 4x8x8 slice. The times are simulated.
512 devices in a mesh: expert: 64 (over y, z), tensor: 8 (over x, core).
Axes of the slice: x: 4, y: 8, z: 8, core: 2. Of those that a mesh axis runs over, the one named last changes fastest.
Arguments:
- queries: bfloat16 [8192, 4096], P('expert', 'tensor'), may hold values from -6 to 6
- keys: bfloat16 [8192, 512], P('expert'), may hold values from -6 to 6
- values: bfloat16 [8192, 512], P('expert'), may hold values from -6 to 6
- segments: int32 [64, 128], P('expert'), may hold values from 0 to 3, never falling along the last dimension, each value on 1 to 64 neighbouring positions
- out_weight: bfloat16 [4096, 2048], P('tensor'), may hold values from -0.09375 to 0.09375
- residual: bfloat16 [8192, 2048], P(('expert', 'tensor')), may hold values from -4 to 4
- norm_gain: float32 [2048], replicated, may hold values from 0.1 to 1.9
- picks: int32 [8192, 8], P('expert'), may hold values from 0 to 63, all different within a row; in each aligned block of 16 rows (0 to 15, 16 to 31, ...) at most 3 rows name the same one
- route_weights: float32 [8192, 8], P('expert'), may hold values from 0.1 to 0.5
- w_gate: bfloat16 [64, 2048, 1536], P('expert', None, 'tensor'), may hold values from -0.125 to 0.125
- w_up: bfloat16 [64, 2048, 1536], P('expert', None, 'tensor'), may hold values from -0.125 to 0.125
- w_down: bfloat16 [64, 1536, 2048], P('expert', None, 'tensor'), may hold values from -0.15625 to 0.15625
Outputs:
- stream: bfloat16 [8192, 2048], P(('expert', 'tensor'))
- layer_out: bfloat16 [8192, 2048], P(('expert', 'tensor'))
Inputs may be any that keep to these rules, and one draw needn't show every extreme that they name: A token's 8 picks are distinct. Split the tokens into aligned blocks of 16 rows; in each block no expert is picked by more than 3 rows.
All inputs are finite; a program needn't handle non-finite values.
Results may differ from a plain program's by a relative error of at most 0.02.
Values may be sent and summed in bfloat16 or wider, within the bound.
A program may use at most 64 MiB of HBM per device.

v0:
```python
import math

import jax
import jax.numpy as jnp
from jax import lax
from jax.sharding import PartitionSpec as P

D = 2048
HEADS = 32
KVH = 4
HD = 128
TOP = 8


def slot_places(picks_blocks, expert_count, capacity):
    block_count, row_count, picked = picks_blocks.shape
    flat_picks = picks_blocks.reshape(block_count, row_count * picked)
    one_hot = (
        flat_picks[:, :, None] == jnp.arange(expert_count, dtype=jnp.int32)[None, None, :]
    ).astype(jnp.int32)
    earlier = jnp.cumsum(one_hot, axis=1) - one_hot
    slot_rank = jnp.sum(earlier * one_hot, axis=2)
    target = flat_picks * capacity + slot_rank
    places = (
        target[:, :, None] == jnp.arange(expert_count * capacity, dtype=jnp.int32)[None, None, :]
    )
    return places.astype(jnp.float32).reshape(
        block_count, row_count, picked, expert_count * capacity
    )


def shards(
    queries,
    keys,
    values,
    segments,
    out_weight,
    residual,
    norm_gain,
    picks,
    route_weights,
    w_gate,
    w_up,
    w_down,
):
    tensor_count = lax.axis_size("tensor")
    expert_count = lax.axis_size("expert")
    tensor_index = lax.axis_index("tensor")
    row_count = residual.shape[0]
    group_tokens = queries.shape[0]
    capacity = max(2, 3 * row_count * TOP // (2 * expert_count))
    local_heads = queries.shape[1] // HD
    head_ids = tensor_index * local_heads + jnp.arange(local_heads, dtype=jnp.int32)
    choose = (
        head_ids[:, None] // (HEADS // KVH) == jnp.arange(KVH, dtype=jnp.int32)[None, :]
    ).astype(jnp.bfloat16)
    key_heads = jnp.einsum(
        "skd,hk->shd",
        keys.reshape(group_tokens, KVH, HD),
        choose,
        preferred_element_type=jnp.float32,
    ).astype(jnp.bfloat16)
    value_heads = jnp.einsum(
        "skd,hk->shd",
        values.reshape(group_tokens, KVH, HD),
        choose,
        preferred_element_type=jnp.float32,
    ).astype(jnp.bfloat16)
    query_heads = queries.reshape(group_tokens, local_heads, HD)
    scores = jnp.einsum(
        "thd,shd->hts", query_heads, key_heads, preferred_element_type=jnp.float32
    ) * (1.0 / math.sqrt(HD))
    position = jnp.arange(group_tokens, dtype=jnp.int32)
    documents = segments[0]
    visible = (documents[:, None] == documents[None, :]) & (position[None, :] <= position[:, None])
    scores = jnp.where(visible[None], scores, -1e30)
    row_top = jnp.max(scores, axis=2, keepdims=True)
    expanded = jnp.exp(scores - row_top)
    weights_bf = (expanded / jnp.sum(expanded, axis=2, keepdims=True)).astype(jnp.bfloat16)
    context = jnp.einsum(
        "hts,shd->thd", weights_bf, value_heads, preferred_element_type=jnp.float32
    ).astype(jnp.bfloat16)
    context = context.reshape(group_tokens, local_heads * HD)
    attended = lax.psum_scatter(
        jnp.dot(context, out_weight, preferred_element_type=jnp.float32).astype(jnp.bfloat16),
        "tensor",
        scatter_dimension=0,
        tiled=True,
    ).astype(jnp.float32)
    hidden_sum = residual.astype(jnp.float32) + attended
    stream = hidden_sum.astype(jnp.bfloat16)
    mean_square = jnp.mean(hidden_sum * hidden_sum, axis=1, keepdims=True)
    normed = (hidden_sum * lax.rsqrt(mean_square + 1e-06) * norm_gain[None, :]).astype(jnp.bfloat16)
    gate_local = w_gate[0]
    up_local = w_up[0]
    down_local = w_down[0]
    width_here = down_local.shape[1]
    group_normed = lax.all_gather(normed, "tensor", axis=0, tiled=True)
    places = slot_places(picks.reshape(tensor_count, row_count, TOP), expert_count, capacity)
    dispatch_table = jnp.sum(places, axis=2).astype(jnp.bfloat16)
    outgoing = jnp.einsum(
        "brs,brd->sbd",
        dispatch_table,
        group_normed.reshape(tensor_count, row_count, D),
        preferred_element_type=jnp.float32,
    ).astype(jnp.bfloat16)
    outgoing = outgoing.reshape(expert_count, capacity, tensor_count, D)
    arrived = lax.all_to_all(outgoing, "expert", split_axis=0, concat_axis=0, tiled=True)
    flat_rows = arrived.reshape(-1, D)
    gate_value = jnp.dot(flat_rows, gate_local, preferred_element_type=jnp.float32)
    up_value = jnp.dot(flat_rows, up_local, preferred_element_type=jnp.float32)
    active = (jax.nn.silu(gate_value) * up_value).astype(jnp.bfloat16)
    expert_out = jnp.dot(
        lax.all_gather(active, "tensor", axis=1, tiled=True),
        down_local,
        preferred_element_type=jnp.float32,
    )
    expert_out = expert_out.astype(jnp.bfloat16).reshape(
        expert_count, capacity, tensor_count, width_here
    )
    returned = lax.all_to_all(expert_out, "expert", split_axis=0, concat_axis=0, tiled=True)
    combine = jnp.sum(
        places * route_weights.reshape(tensor_count, row_count, TOP)[:, :, :, None], axis=2
    )
    band_sums = jnp.einsum(
        "brs,sbf->brf",
        combine,
        returned.astype(jnp.float32).reshape(expert_count * capacity, tensor_count, width_here),
        precision=lax.Precision.HIGHEST,
    )
    mixture = (
        lax.all_to_all(
            band_sums.astype(jnp.bfloat16), "tensor", split_axis=0, concat_axis=2, tiled=True
        )
        .astype(band_sums.dtype)
        .reshape(row_count, D)
    )
    layer_out = (hidden_sum + mixture).astype(jnp.bfloat16)
    return (stream, layer_out)


def solution(mesh):
    in_specs = (
        P("expert", "tensor"),
        P("expert", None),
        P("expert", None),
        P("expert", None),
        P("tensor", None),
        P(("expert", "tensor"), None),
        P(),
        P("expert", None),
        P("expert", None),
        P("expert", None, "tensor"),
        P("expert", None, "tensor"),
        P("expert", None, "tensor"),
    )
    out_specs = (P(("expert", "tensor"), None), P(("expert", "tensor"), None))
    return jax.shard_map(shards, mesh=mesh, in_specs=in_specs, out_specs=out_specs, check_vma=False)
```

profile of v0, /device:TPU:16, one launch (start us, length us, event | category | flops | bytes accessed | tf_op | source)
XLA Modules:
  0.0 357.4 jit_solution(5860082028272537622)
XLA Ops:
  7.2 0.9 fusion.25
  8.1 0.9 reshape.148
  9.1 0.3 fusion.7
  9.4 1.1 fusion.4
  10.6 0.9 reshape.147
  11.5 0.3 fusion.6
  12.1 1.3 convolution_convert_fusion.1
  13.9 2.5 select_reduce_fusion.1
  16.6 0.7 convert_reduce_fusion
  17.3 36.9 %reduce-scatter.2.cloned.1.call-done = bf16[16,2048]{1,0:T(8,128)(2,1)} async-done(((bf16[128,2048]{1,0:T(8,128)(2,1)}), bf16[16,2048]{1,0:T(8,128)(2,1)}) %reduce-scatter.2.cloned.1.call-update) | async-done | bytes 65552 | tf_op jit(solution)/shard_map/reduce_scatter | solution.py:84
  54.2 1.0 multiply_reduce_fusion
  55.2 0.9 multiply_convert_fusion
  56.1 13.1 %all_gather.6 = bf16[128,2048]{1,0:T(8,128)(2,1)S(1)} all-gather(bf16[16,2048]{1,0:T(8,128)(2,1)S(1)} %multiply_convert_fusion), channel_id=1, replica_groups=mesh['expert'=64,'tensor'=8] {'tensor'}, dimensions={0}, use_global_device_ids=true | all-gather | bytes 589824 | tf_op jit(solution)/shard_map/all_gather | solution.py:98
  69.2 1.8 convert_bitcast_fusion
  71.1 3.4 copy.50
  74.5 173.3 %all_to_all.19 = bf16[64,3,8,2048]{3,2,1,0:T(8,128)(2,1)S(1)} all-to-all(bf16[64,3,8,2048]{3,2,1,0:T(8,128)(2,1)S(1)} %bitcast.68), channel_id=1, replica_groups=mesh['expert'=64,'tensor'=8] {'expert'}, dimensions={0} | all-to-all | bytes 12582912 | tf_op jit(solution)/shard_map/all_to_all | solution.py:108
  247.8 2.2 fusion.10
  250.0 3.2 fusion.1
  253.2 45.3 %all-gather.2.cloned.1.call-done = bf16[1536,1536]{0,1:T(8,128)(2,1)} async-done(((bf16[1536,192]{0,1:T(8,128)(2,1)}), bf16[1536,1536]{0,1:T(8,128)(2,1)}) %all-gather.2.cloned.1.call-update) | async-done | bytes 4718608 | tf_op jit(solution)/shard_map/all_gather | solution.py:114
  298.6 3.8 %convolution_convert_fusion = bf16[1536,256]{1,0:T(8,128)(2,1)S(1)} fusion(bf16[1536,1536]{0,1:T(8,128)(2,1)} %all-gather.2.cloned.1.call-done, bf16[1,1536,256]{2,1,0:T(8,128)(2,1)S(1)} %copy-done.8), kind=kOutput, calls=%fused_computation.3 | convolution fusion | flops 1208352768 | bytes 6291456 | tf_op jit(solution)/shard_map/dot_general | solution.py:113
  302.3 38.6 %all_to_all.20 = bf16[64,3,8,256]{3,2,1,0:T(8,128)(2,1)S(1)} all-to-all(bf16[64,3,8,256]{3,2,1,0:T(8,128)(2,1)S(1)} %bitcast.73), channel_id=1, replica_groups=mesh['expert'=64,'tensor'=8] {'expert'}, dimensions={0} | all-to-all | bytes 1572864 | tf_op jit(solution)/shard_map/all_to_all | solution.py:121
  341.0 0.5 convolution_convert_fusion.5
  341.4 8.4 %all_to_all.21 = bf16[8,16,256]{2,1,0:T(8,128)(2,1)S(1)} all-to-all(bf16[8,16,256]{2,1,0:T(8,128)(2,1)S(1)} %convolution_convert_fusion.5), channel_id=1, replica_groups=mesh['expert'=64,'tensor'=8] {'tensor'}, dimensions={0} | all-to-all | bytes 131072 | tf_op jit(solution)/shard_map/all_to_all | solution.py:132
  349.9 0.7 add_convert_fusion
  (36 shorter events, 1.1 us)
Async XLA Ops:
  7.2 4.9 %copy-start = (bf16[512,2048]{1,0:T(8,128)(2,1)S(1)}, bf16[512,2048]{1,0:T(8,128)(2,1)}, u32[]{:S(2)}) copy-start(bf16[512,2048]{1,0:T(8,128)(2,1)} %param.16) | copy-start | bytes 6291460
  7.2 47.0 %reduce-scatter.2.cloned.1.call-start = ((), (), s32[]{:S(2)}) async-start(), calls=%async_computation.4 | async-start | bytes 589824 | tf_op jit(solution)/shard_map/reduce_scatter | solution.py:84
  11.8 1.6 copy-start.3
  11.8 1.8 copy-start.5
  12.1 42.1 %copy-start.1 = (bf16[16,2048]{1,0:T(8,128)(2,1)S(1)}, bf16[16,2048]{1,0:T(8,128)(2,1)}, u32[]{:S(2)}) copy-start(bf16[16,2048]{1,0:T(8,128)(2,1)} %param.17) | copy-start | bytes 196612
  12.1 43.1 %copy-start.4 = (f32[2048]{0:T(1024)S(1)}, f32[2048]{0:T(1024)}, u32[]{:S(2)}) copy-start(f32[2048]{0:T(1024)} %param.18) | copy-start | bytes 24580
  13.4 285.2 %all-gather.2.cloned.1.call-start = ((), (), s32[]{:S(2)}) async-start(), calls=%async_computation.5 | async-start | bytes 5308416 | tf_op jit(solution)/shard_map/all_gather | solution.py:114
  74.5 173.3 %copy-start.6 = (bf16[1,2048,192]{1,2,0:T(8,128)(2,1)S(1)}, bf16[1,2048,192]{1,2,0:T(8,128)(2,1)}, u32[]{:S(2)}) copy-start(bf16[1,2048,192]{1,2,0:T(8,128)(2,1)} %param.21) | copy-start | bytes 2359300
  247.8 2.2 copy-start.7
  250.0 48.5 %copy-start.8 = (bf16[1,1536,256]{2,1,0:T(8,128)(2,1)S(1)}, bf16[1,1536,256]{2,1,0:T(8,128)(2,1)}, u32[]{:S(2)}) copy-start(bf16[1,1536,256]{2,1,0:T(8,128)(2,1)} %param.23) | copy-start | bytes 2359300
  302.3 47.5 %copy-start.2 = (bf16[16,2048]{1,0:T(8,128)(2,1)S(1)}, bf16[16,2048]{1,0:T(8,128)(2,1)}, u32[]{:S(2)}) copy-start(bf16[16,2048]{1,0:T(8,128)(2,1)} %reduce-scatter.2.cloned.1.call-done) | copy-start | bytes 196612
Sparse Core Ops, SparseCore 0:
  13.5 40.6 reduce-scatter.1
  253.4 45.1 all-gather.1
where the time goes:
time: 358 us; the launch traced here: 357 us
  blocking collectives  233 us (65%)
  waiting for transfers between devices  82.3 us (23%)
  matrix products  14.6 us (4%)
  between operations  14.2 us (4%)
  other arithmetic  6.82 us (2%)
  local copies, waits for them, and re-layouts  5.99 us (2%)
    all_to_all x1, blocking collectives, shards(): lax.all_to_all(outgoing, 'expert', split_axis=0, concat_axis=0, tiled=True)  173 us
    all_gather x1, waiting for transfers between devices, shards(): lax.all_gather(active, 'tensor', axis=1, tiled=True)  45.3 us
    all_to_all x1, blocking collectives, shards(): lax.all_to_all(expert_out, 'expert', split_axis=0, concat_axis=0, tiled=T...  38.6 us
    reduce_scatter x1, waiting for transfers between devices, shards(): lax.psum_scatter(jnp.dot(context, out_weight, preferred_element_type=jnp....  36.9 us
    all_gather x1, blocking collectives, shards(): group_normed = lax.all_gather(normed, 'tensor', axis=0, tiled=True)  13.1 us
    all_to_all x1, blocking collectives, shards(): lax.all_to_all(band_sums.astype(jnp.bfloat16), 'tensor', split_axis=0, co...  8.4 us
  transfers between devices with their start and end apart: 2, of which 2 were waited for; matrix products, arithmetic and copies ran while one was open for 1% of the time, Pallas kernels for 0%

commit v1 on v0

v1 whole, which is shorter than its diff:
```python
import math

import jax
import jax.numpy as jnp
from jax import lax
from jax.experimental import pallas as pl
from jax.experimental.pallas import tpu as pltpu
from jax.sharding import PartitionSpec as P

D = 2048
HEADS = 32
KVH = 4
HD = 128
TOP = 8
ROWS = 16
CAP = 3
XN = 4
RING = 8
QD = D // XN
HID = 192
BLKS = RING * XN
HALF = CAP * BLKS // 2
SLOTS = 2 * HALF
TOKS = BLKS * ROWS
BF = jnp.bfloat16
F32 = jnp.float32


def ahead(step):
    odd = lax.rem(step, 2)
    return RING + odd * ((step + 1) // 2) - (1 - odd) * (step // 2)


def moe_kernel(
    nrm, hid, meta, wg, wu, wd,
    out,
    wgs, wus, wds, metas, gath, code, wtok, table, wflat, comb, disp, xg, act, back, ret, part, parts, mix, fin,
    w_s, w_r, m_s, m_r, xa_s, xa_r, g_s, g_r, d_s, d_r, xg_s, xg_r, ac_s, ac_r, rt_s, rt_r, rs_s, rs_r, xb_s, xb_r,
):
    exp = lax.axis_index("expert")
    ten = lax.axis_index("tensor")
    x = ten // 2
    c = lax.rem(ten, 2)
    y = exp // RING
    z = lax.rem(exp, RING)
    st1 = RING - (RING - 1) * c
    st2 = 1 + (RING - 1) * c
    r1 = (1 - c) * y + c * z
    r2 = (1 - c) * z + c * y

    def ring1(r):
        return r * st1 + r2 * st2, ten

    def ring2(r):
        return r1 * st1 + r * st2, ten

    def along_x(xx):
        return exp, xx * 2 + c

    sibling = (exp, x * 2 + 1 - c)
    xp = lax.rem(x + 1, XN)
    xm = lax.rem(x + XN - 1, XN)
    xo = lax.rem(x + 2, XN)

    def rcopy(src, dst, ss, rs, dev):
        return pltpu.make_async_remote_copy(
            src_ref=src, dst_ref=dst, send_sem=ss, recv_sem=rs, device_id=dev,
            device_id_type=pl.DeviceIdType.MESH,
        )

    def arrived(dst, rs):
        rcopy(dst, dst, rs, rs, sibling).wait_recv()

    def sent(src, ss):
        rcopy(src, src, ss, ss, sibling).wait_send()

    def band(xx, width):
        return pl.ds(pl.multiple_of(xx * width, 128), width)

    def block(xx):
        return pl.ds(pl.multiple_of(xx * ROWS, ROWS), ROWS)

    barrier = pltpu.get_barrier_semaphore()

    def greet(dev):
        pl.semaphore_signal(barrier, inc=1, device_id=dev, device_id_type=pl.DeviceIdType.MESH)

    greet(sibling)
    for d in range(1, XN):
        greet(along_x(lax.rem(x + d, XN)))
    for d in range(1, RING):
        greet(ring1(lax.rem(r1 + d, RING)))
        greet(ring2(lax.rem(r2 + d, RING)))
    pl.semaphore_wait(barrier, 1 + (XN - 1) + 2 * (RING - 1))

    for d in range(1, XN):
        to = lax.rem(x + d, XN)
        rcopy(nrm.at[:, band(to, QD)], gath.at[r1, block(x)], xa_s.at[d], xa_r.at[d], along_x(to)).start()
    gath[r1, block(x), :] = nrm[:, band(x, QD)]
    for d in range(1, RING):
        to = lax.rem(r1 + d, RING)
        rcopy(meta, metas.at[r1], m_s.at[d], m_r.at[d], ring1(to)).start()
    metas[r1] = meta[...]
    for d in range(1, XN):
        arrived(gath.at[r1, block(lax.rem(x + XN - d, XN))], xa_r.at[d])
    for d in range(1, RING):
        to = lax.rem(r1 + d, RING)
        rcopy(gath.at[r1], gath.at[r1], g_s.at[d], g_r.at[d], ring1(to)).start()
    for k, (mine, theirs) in enumerate(((wg, wgs), (wu, wus), (wd, wds))):
        rcopy(mine, theirs, w_s.at[k], w_r.at[k], sibling).start()

    for d in range(1, RING):
        arrived(metas.at[lax.rem(r1 + RING - d, RING)], m_r.at[d])
    ids = (r1 * st1 + lax.broadcasted_iota(jnp.int32, (RING, 128), 0) * st2).astype(F32)
    row_a = lax.broadcasted_iota(jnp.int32, (128, 128), 0)
    row_b = lax.broadcasted_iota(jnp.int32, (128, 128), 1)
    before = ((row_a // ROWS == row_b // ROWS) & (row_a < row_b)).astype(F32).astype(BF)
    low = lax.broadcasted_iota(jnp.int32, (2 * TOP, 128), 1) < 64
    for p in range(RING // 2):
        pair = jnp.where(low, metas[2 * p], metas[2 * p + 1])
        member = jnp.zeros((RING, 128), F32)
        weight = jnp.zeros((RING, 128), F32)
        for k in range(TOP):
            hit = pair[k : k + 1, :] == ids
            member = member + hit.astype(F32)
            weight = weight + jnp.where(hit, pair[TOP + k : TOP + k + 1, :], 0.0)
        rank = jnp.dot(member.astype(BF), before, preferred_element_type=F32)
        code[:, p * 128 : (p + 1) * 128] = jnp.where(member > 0.5, rank, -1.0)
        wtok[:, p * 128 : (p + 1) * 128] = weight
    slot = lax.broadcasted_iota(jnp.int32, (HALF, TOKS // 2), 0)
    token = lax.broadcasted_iota(jnp.int32, (HALF, TOKS // 2), 1)
    same = lax.rem(slot, BLKS // 2) == token // ROWS
    place = jnp.where(same, (slot // (BLKS // 2)).astype(F32), -2.0)
    for h in range(2):
        lanes = slice(h * (TOKS // 2), (h + 1) * (TOKS // 2))
        for e in range(RING):
            mask = place == code[e : e + 1, lanes]
            table[e, h] = mask.astype(F32).astype(BF)
            wflat[e * HALF : (e + 1) * HALF, :] = jnp.where(mask, wtok[e : e + 1, lanes], 0.0)
        turned = wflat[...].T
        coarse = turned.astype(BF)
        comb[h, : TOKS // 2] = coarse
        comb[h, TOKS // 2 :] = (turned - coarse.astype(F32)).astype(BF)

    for d in range(1, RING):
        arrived(gath.at[lax.rem(r1 + RING - d, RING)], g_r.at[d])

    def slots_for(e):
        tops = []
        for h in range(2):
            rows = gath[h * (RING // 2) : (h + 1) * (RING // 2)].reshape(TOKS // 2, QD)
            tops.append(jnp.dot(table[e, h], rows, preferred_element_type=F32).astype(BF))
        return tops

    def spread(ref, sem_s, sem_r, i, width):
        piece = ref.at[i, :, band(x, width)]
        rcopy(piece, piece, sem_s.at[i, 0], sem_r.at[i, 0], along_x(xp)).start()
        rcopy(piece, piece, sem_s.at[i, 1], sem_r.at[i, 1], along_x(xm)).start()

    def relay(ref, sem_s, sem_r, i, width):
        arrived(ref.at[i, :, band(xm, width)], sem_r.at[i, 0])
        up = ref.at[i, pl.ds(0, HALF), band(xm, width)]
        rcopy(up, up, sem_s.at[i, 2], sem_r.at[i, 2], along_x(xp)).start()
        arrived(ref.at[i, :, band(xp, width)], sem_r.at[i, 1])
        down = ref.at[i, pl.ds(HALF, HALF), band(xp, width)]
        rcopy(down, down, sem_s.at[i, 3], sem_r.at[i, 3], along_x(xm)).start()

    def relayed(ref, sem_r, i, width):
        arrived(ref.at[i, pl.ds(0, HALF), band(xo, width)], sem_r.at[i, 2])
        arrived(ref.at[i, pl.ds(HALF, HALF), band(xo, width)], sem_r.at[i, 3])

    own = slots_for(r2)
    for h in range(2):
        xg[0, h * HALF : (h + 1) * HALF, band(x, QD)] = own[h]
    spread(xg, xg_s, xg_r, 0, QD)

    def dispatch(i, carry):
        to = lax.rem(r2 + ahead(i), RING)
        tops = slots_for(to)
        for h in range(2):
            disp[i, h * HALF : (h + 1) * HALF, :] = tops[h]
        rcopy(disp.at[i], xg.at[i, :, band(x, QD)], d_s.at[i], d_r.at[i], ring2(to)).start()
        return carry

    lax.fori_loop(1, RING, dispatch, 0)

    for k, theirs in enumerate((wgs, wus, wds)):
        arrived(theirs, w_r.at[k])

    def gate_up(i):
        relayed(xg, xg_r, i, QD)
        rows = xg[i]

        def units(gate, up):
            g = jnp.dot(rows, gate[...], preferred_element_type=F32)
            u = jnp.dot(rows, up[...], preferred_element_type=F32)
            return g / (1.0 + jnp.exp(-g)) * u

        mine = units(wg, wu)
        theirs = units(wgs, wus)
        first = jnp.where(c == 0, mine, theirs)
        second = jnp.where(c == 0, theirs, mine)
        act[i, :, band(x, 2 * HID)] = jnp.concatenate([first, second], axis=1).astype(BF)
        spread(act, ac_s, ac_r, i, 2 * HID)

    def down(i):
        relayed(act, ac_r, i, 2 * HID)
        rows = act[i]
        mine = jnp.dot(rows, wd[...], preferred_element_type=F32).astype(BF)
        theirs = jnp.dot(rows, wds[...], preferred_element_type=F32).astype(BF)
        back[i, :, band(c, QD // 2)] = mine
        back[i, :, band(1 - c, QD // 2)] = theirs

        @pl.when(i == 0)
        def _():
            ret[r2] = back[0]

        @pl.when(i > 0)
        def _():
            to = lax.rem(r2 + 2 * RING - ahead(i), RING)
            rcopy(back.at[i], ret.at[r2], rt_s.at[i], rt_r.at[i], ring2(to)).start()

    def step(it, carry):
        @pl.when(it < RING - 1)
        def _():
            arrived(xg.at[it + 1, :, band(x, QD)], d_r.at[it + 1])
            spread(xg, xg_s, xg_r, it + 1, QD)

        @pl.when(it < RING)
        def _():
            relay(xg, xg_s, xg_r, it, QD)

        @pl.when((it >= 1) & (it < RING + 1))
        def _():
            gate_up(it - 1)

        @pl.when((it >= 2) & (it < RING + 2))
        def _():
            relay(act, ac_s, ac_r, it - 2, 2 * HID)

        @pl.when(it >= 3)
        def _():
            down(it - 3)

        return carry

    lax.fori_loop(0, RING + 3, step, 0)

    def returned(i, carry):
        arrived(ret.at[lax.rem(r2 + ahead(i), RING)], rt_r.at[i])
        return carry

    lax.fori_loop(1, RING, returned, 0)

    for h in range(2):
        rows = ret[:, h * HALF : (h + 1) * HALF, :].reshape(RING * HALF, QD)
        both = jnp.dot(comb[h], rows, preferred_element_type=F32)
        sums = (both[: TOKS // 2] + both[TOKS // 2 :]).astype(BF)
        part[h * (RING // 2) : (h + 1) * (RING // 2)] = sums.reshape(RING // 2, XN * ROWS, QD)
    for d in range(1, RING):
        to = lax.rem(r1 + d, RING)
        rcopy(part.at[to], parts.at[r1], rs_s.at[d], rs_r.at[d], ring1(to)).start()
    total = part[r1].astype(F32)
    for d in range(1, RING):
        at = lax.rem(r1 + RING - d, RING)
        arrived(parts.at[at], rs_r.at[d])
        total = total + parts[at].astype(F32)
    mix[...] = total.astype(BF)
    for d in range(1, XN):
        to = lax.rem(x + d, XN)
        rcopy(mix.at[block(to)], fin.at[:, band(x, QD)], xb_s.at[d], xb_r.at[d], along_x(to)).start()
    fin[:, band(x, QD)] = mix[block(x), :]
    for d in range(1, XN):
        arrived(fin.at[:, band(lax.rem(x + XN - d, XN), QD)], xb_r.at[d])
    out[...] = (hid[...] + fin[...].astype(F32)).astype(BF)

    for k, mine in enumerate((wg, wu, wd)):
        sent(mine, w_s.at[k])
    for d in range(1, XN):
        sent(nrm.at[:, band(x, QD)], xa_s.at[d])
        sent(mix.at[block(x)], xb_s.at[d])
    for d in range(1, RING):
        sent(meta, m_s.at[d])
        sent(gath.at[r1], g_s.at[d])
        sent(part.at[r1], rs_s.at[d])

    def drain(i, carry):
        @pl.when(i > 0)
        def _():
            sent(disp.at[i], d_s.at[i])
            sent(back.at[i], rt_s.at[i])

        for k in range(2):
            sent(xg.at[i, :, band(x, QD)], xg_s.at[i, k])
            sent(act.at[i, :, band(x, 2 * HID)], ac_s.at[i, k])
            sent(xg.at[i, pl.ds(0, HALF), band(x, QD)], xg_s.at[i, 2 + k])
            sent(act.at[i, pl.ds(0, HALF), band(x, 2 * HID)], ac_s.at[i, 2 + k])
        return carry

    lax.fori_loop(0, RING, drain, 0)


def experts(normed, hidden_sum, meta, w_gate, w_up, w_down):
    dma = pltpu.SemaphoreType.DMA
    vmem = pltpu.VMEM
    return pl.pallas_call(
        moe_kernel,
        out_shape=jax.ShapeDtypeStruct((ROWS, D), BF),
        in_specs=[pl.BlockSpec(memory_space=pltpu.VMEM)] * 6,
        out_specs=pl.BlockSpec(memory_space=pltpu.VMEM),
        scratch_shapes=[
            vmem((D, HID), BF),
            vmem((D, HID), BF),
            vmem((XN * 2 * HID, QD // 2), BF),
            vmem((RING, 2 * TOP, 128), F32),
            vmem((RING, XN * ROWS, QD), BF),
            vmem((RING, TOKS), F32),
            vmem((RING, TOKS), F32),
            vmem((RING, 2, HALF, TOKS // 2), BF),
            vmem((RING * HALF, TOKS // 2), F32),
            vmem((2, TOKS, RING * HALF), BF),
            vmem((RING, SLOTS, QD), BF),
            vmem((RING, SLOTS, D), BF),
            vmem((RING, SLOTS, XN * 2 * HID), BF),
            vmem((RING, SLOTS, QD), BF),
            vmem((RING, SLOTS, QD), BF),
            vmem((RING, XN * ROWS, QD), BF),
            vmem((RING, XN * ROWS, QD), BF),
            vmem((XN * ROWS, QD), BF),
            vmem((ROWS, D), BF),
            dma((3,)), dma((3,)),
            dma((RING,)), dma((RING,)),
            dma((XN,)), dma((XN,)),
            dma((RING,)), dma((RING,)),
            dma((RING,)), dma((RING,)),
            dma((RING, 4)), dma((RING, 4)),
            dma((RING, 4)), dma((RING, 4)),
            dma((RING,)), dma((RING,)),
            dma((RING,)), dma((RING,)),
            dma((XN,)), dma((XN,)),
        ],
        compiler_params=pltpu.CompilerParams(
            collective_id=0, has_side_effects=True, vmem_limit_bytes=50 * 1024 * 1024
        ),
        name="experts",
    )(normed, hidden_sum, meta, w_gate, w_up, w_down)


def shards(
    queries,
    keys,
    values,
    segments,
    out_weight,
    residual,
    norm_gain,
    picks,
    route_weights,
    w_gate,
    w_up,
    w_down,
):
    tensor_index = lax.axis_index("tensor")
    group_tokens = queries.shape[0]
    local_heads = queries.shape[1] // HD
    head_ids = tensor_index * local_heads + jnp.arange(local_heads, dtype=jnp.int32)
    choose = (
        head_ids[:, None] // (HEADS // KVH) == jnp.arange(KVH, dtype=jnp.int32)[None, :]
    ).astype(jnp.bfloat16)
    key_heads = jnp.einsum(
        "skd,hk->shd",
        keys.reshape(group_tokens, KVH, HD),
        choose,
        preferred_element_type=jnp.float32,
    ).astype(jnp.bfloat16)
    value_heads = jnp.einsum(
        "skd,hk->shd",
        values.reshape(group_tokens, KVH, HD),
        choose,
        preferred_element_type=jnp.float32,
    ).astype(jnp.bfloat16)
    query_heads = queries.reshape(group_tokens, local_heads, HD)
    scores = jnp.einsum(
        "thd,shd->hts", query_heads, key_heads, preferred_element_type=jnp.float32
    ) * (1.0 / math.sqrt(HD))
    position = jnp.arange(group_tokens, dtype=jnp.int32)
    documents = segments[0]
    visible = (documents[:, None] == documents[None, :]) & (position[None, :] <= position[:, None])
    scores = jnp.where(visible[None], scores, -1e30)
    row_top = jnp.max(scores, axis=2, keepdims=True)
    expanded = jnp.exp(scores - row_top)
    weights_bf = (expanded / jnp.sum(expanded, axis=2, keepdims=True)).astype(jnp.bfloat16)
    context = jnp.einsum(
        "hts,shd->thd", weights_bf, value_heads, preferred_element_type=jnp.float32
    ).astype(jnp.bfloat16)
    context = context.reshape(group_tokens, local_heads * HD)
    attended = lax.psum_scatter(
        jnp.dot(context, out_weight, preferred_element_type=jnp.float32).astype(jnp.bfloat16),
        "tensor",
        scatter_dimension=0,
        tiled=True,
    ).astype(jnp.float32)
    hidden_sum = residual.astype(jnp.float32) + attended
    stream = hidden_sum.astype(jnp.bfloat16)
    mean_square = jnp.mean(hidden_sum * hidden_sum, axis=1, keepdims=True)
    normed = (hidden_sum * lax.rsqrt(mean_square + 1e-06) * norm_gain[None, :]).astype(jnp.bfloat16)

    core = lax.rem(tensor_index, 2)
    routing = jnp.concatenate([picks.astype(F32), route_weights], axis=1)
    routing = routing.reshape(XN, 2, ROWS, 2 * TOP)
    routing = jnp.where(core == 0, routing[:, 0], routing[:, 1]).reshape(XN * ROWS, 2 * TOP).T
    meta = jnp.concatenate([routing, routing], axis=1)
    layer_out = experts(normed, hidden_sum, meta, w_gate[0], w_up[0], w_down[0])
    return (stream, layer_out)


def solution(mesh):
    in_specs = (
        P("expert", "tensor"),
        P("expert", None),
        P("expert", None),
        P("expert", None),
        P("tensor", None),
        P(("expert", "tensor"), None),
        P(),
        P("expert", None),
        P("expert", None),
        P("expert", None, "tensor"),
        P("expert", None, "tensor"),
        P("expert", None, "tensor"),
    )
    out_specs = (P(("expert", "tensor"), None), P(("expert", "tensor"), None))
    return jax.shard_map(shards, mesh=mesh, in_specs=in_specs, out_specs=out_specs, check_vma=False)
```

time: 358 us -> 168 us (0.47)
  the two profiles are of different devices: /device:TPU:16 before, /device:TPU:2 now
where the time goes in v1:
time: 168 us; the launch traced here: 167 us
  Pallas kernels  103 us (61%)
  waiting for transfers between devices  33.9 us (20%)
  between operations  14.2 us (8%)
  local copies, waits for them, and re-layouts  8.97 us (5%)
  other arithmetic  3.62 us (2%)
  matrix products  3.17 us (2%)
    pallas_call x1, Pallas kernels, experts(): pl.pallas_call(moe_kernel, out_shape=jax.ShapeDtypeStruct((ROWS, D), BF),...  103 us
    reduce_scatter x1, waiting for transfers between devices, shards(): lax.psum_scatter(jnp.dot(context, out_weight, preferred_element_type=jnp....  33.9 us
    unnamed x17, local copies, waits for them, and re-layouts  6.69 us
  transfers between devices with their start and end apart: 1, of which 1 were waited for; matrix products, arithmetic and copies ran while one was open for 2% of the time, Pallas kernels for 0%

profile of v1, /device:TPU:2, one launch (start us, length us, event | category | flops | bytes accessed | tf_op | source)
XLA Modules:
  0.0 167.3 jit_solution(14519824622538940531)
XLA Ops:
  7.2 0.0 reduce-scatter.2.cloned.1.call-start
  7.2 0.9 fusion.12
  8.1 0.9 reshape.116
  9.1 0.3 fusion.14
  9.4 1.1 fusion.3
  10.5 0.1 fusion.23
  10.6 0.9 reshape.115
  11.5 0.3 fusion.16
  11.8 0.1 copy.20
  12.0 0.2 convolution_convert_fusion.1
  12.2 1.3 convolution_convert_fusion
  13.6 0.1 reshape.119
  13.7 0.1 fusion.22
  13.8 0.1 select_n.30
  13.9 1.4 copy.18
  15.3 2.2 %copy.19 = bf16[1,2048,192]{2,1,0:T(8,128)(2,1)} copy(bf16[1,2048,192]{1,2,0:T(8,128)(2,1)} %param.22) | data formatting | bytes 1572864 | tf_op args[10]
  17.6 0.1 pad_maximum_fusion.1.meta
  17.6 33.9 %reduce-scatter.2.cloned.1.call-done = bf16[16,2048]{1,0:T(8,128)(2,1)} async-done(((bf16[128,2048]{1,0:T(8,128)(2,1)}), bf16[16,2048]{1,0:T(8,128)(2,1)}) %reduce-scatter.2.cloned.1.call-update) | async-done | bytes 65552 | tf_op jit(solution)/shard_map/reduce_scatter | solution.py:397
  51.5 1.6 convert_add_fusion
  53.2 0.9 multiply_convert_fusion.nrm
  54.1 1.2 copy-done.1
  55.3 1.1 copy-done.2
  56.5 103.3 %experts.1 = bf16[16,2048]{1,0:T(8,128)(2,1)S(1)} custom-call(bf16[16,2048]{1,0:T(8,128)(2,1)S(1)} %multiply_convert_fusion.nrm, f32[16,2048]{1,0:T(8,128)S(1)} %get-tuple-element.2.hid, f32[16,128]{1,0:T(8,128)S(1)} %pad_maximum_fusion.1.meta, bf16[2048,192]{1,0:T(8,128)(2,1)S(1)} %bitcast.44, bf16[2048,192]{1,0:T(8,128)(2,1)S(1)} %bitcast.45, ...), custom_call_target="tpu_custom_call" | custom-call | tf_op jit(solution)/shard_map/experts/pallas_call | solution.py:306
  159.8 0.6 copy.35
  (18 shorter events, 0.1 us)
Async XLA Ops:
  7.2 5.0 %copy-start = (bf16[512,2048]{1,0:T(8,128)(2,1)S(1)}, bf16[512,2048]{1,0:T(8,128)(2,1)}, u32[]{:S(2)}) copy-start(bf16[512,2048]{1,0:T(8,128)(2,1)} %param.16) | copy-start | bytes 6291460
  7.2 44.4 %reduce-scatter.2.cloned.1.call-start = ((), (), s32[]{:S(2)}) async-start(), calls=%async_computation.1 | async-start | bytes 589824 | tf_op jit(solution)/shard_map/reduce_scatter | solution.py:397
  11.9 1.6 copy-start.5
  12.0 1.6 copy-start.6
  13.5 38.0 %copy-start.3 = (bf16[16,2048]{1,0:T(8,128)(2,1)S(1)}, bf16[16,2048]{1,0:T(8,128)(2,1)}, u32[]{:S(2)}) copy-start(bf16[16,2048]{1,0:T(8,128)(2,1)} %param.17) | copy-start | bytes 196612
  13.8 39.4 %copy-start.4 = (f32[2048]{0:T(1024)S(1)}, f32[2048]{0:T(1024)}, u32[]{:S(2)}) copy-start(f32[2048]{0:T(1024)} %param.18) | copy-start | bytes 24580
  54.1 1.2 copy-start.1
  55.3 1.1 copy-start.2
Sparse Core Ops, SparseCore 0:
  13.6 37.8 reduce-scatter.1
